TPU v7x, 32 devices: a whole 2x2x4 slice. The times are simulated.
32 devices in a mesh: grp: 2 (over core), blk: 8 (over z, x), real: 2 (over y).
Axes of the slice: x: 2, y: 2, z: 4, core: 2. Of those that a mesh axis runs over, the one named last changes fastest.
Arguments:
- sky_data: float32 [32, 16, 8192], P('real', 'blk', 'grp'), may hold values from -6 to 6
- signal_prev: float32 [32, 16, 8192], P('real', 'blk', 'grp'), may hold values from -6 to 6
- noise_var: float32 [16, 8192], P('blk', 'grp'), may hold values from 1 to 16
- mask_flags: int32 [16, 8192], P('blk', 'grp'), may hold values 0 or 1
- cycle_table: int32 [16], P('blk'), may hold values from 0 to 15, each once
- m_table: int32 [32], replicated, may hold values from 0 to 4095, as said below
- spectrum: float32 [4096], P(('grp', 'real')), may hold values from 0.05 to 5
- legendre: bfloat16 [32, 4096, 16], P('blk', ('grp', 'real')), may hold values from -1.5 to 1.5
Outputs:
- wiener_alm: float32 [32, 2, 32, 4096], P(None, None, 'blk', ('grp', 'real'))
- signal_next: float32 [32, 16, 8192], P('real', 'blk', 'grp')
Inputs may be any that keep to these rules, and one draw needn't show every extreme that they name: `m_table`: distinct orders; 0 and 4095 are always among them. `cycle_table`: each cycle number once.
All inputs are finite; a program needn't handle non-finite values. No bound on the sum of `mask_flags` on one device may be relied on, other than what follows from the above.
Results may differ from a plain program's by a relative error of at most 0.0063.
Values may be sent and summed in bfloat16 or wider, within the bound.
No kernel may reach another device: no remote copies, remote signals or barrier semaphores. Data moves between devices by JAX's collectives and lax.ppermute only.
A program may use at most 64 MiB of HBM per device.

v0:
```python
import functools
import math

import jax
import jax.numpy as jnp
from jax import lax
from jax.experimental import pallas as pl
from jax.experimental.pallas import tpu as pltpu
from jax.sharding import PartitionSpec as P

LANES = 128
NT = (((1,), (1,)), ((), ()))
AXES = ("grp", "blk", "real")
PARTS = 2
FORWARD_VMEM = 32 << 20
BACKWARD_VMEM = 16 << 20


def unit_cosine(units, half_turn):
    wrapped = units & (2 * half_turn - 1)
    folded = jnp.minimum(wrapped, 2 * half_turn - wrapped)
    y = (half_turn // 2 - folded).astype(jnp.float32) * (math.pi / half_turn)
    y2 = y * y
    acc = jnp.full_like(y2, -1.0 / math.factorial(11))
    for order, sign in ((9, 1.0), (7, -1.0), (5, 1.0), (3, -1.0), (1, 1.0)):
        acc = acc * y2 + sign / math.factorial(order)
    return acc * y


def log2(size):
    return size.bit_length() - 1


def lane_ids(shape):
    return lax.broadcasted_iota(jnp.int32, shape, len(shape) - 1)


def row_ids(shape):
    return lax.broadcasted_iota(jnp.int32, shape, len(shape) - 2)


def phase_factors(cycles, orders, cycle_len, half_len, group):
    modes = orders.shape[1]
    orders = jnp.concatenate([orders] * (LANES // modes), axis=1)
    quarter = lane_ids((1, LANES)) >> log2(modes)
    quarter_turn = cycle_len // 2
    row = row_ids((2 * LANES, LANES))
    pixel = (row >> log2(LANES)) * (half_len // 2) + (row & (LANES - 1))
    inner_units = 2 * orders * pixel + ((quarter + 1) >> 1) * quarter_turn
    inner = unit_cosine(inner_units, cycle_len)
    rows = half_len // LANES
    row = row_ids((rows, LANES))
    parity = jnp.where((row & 1) == 0, cycles[:, :1], cycles[:, 1:]) & 1
    pixel = group * half_len + LANES * (row >> 1)
    outer_units = orders * (2 * pixel + parity) + (quarter >> 1) * (3 * quarter_turn)
    outer = unit_cosine(outer_units, cycle_len)
    high = inner.astype(jnp.bfloat16)
    low = (inner - high.astype(jnp.float32)).astype(jnp.bfloat16)
    return jnp.concatenate([high, low], axis=1), outer


def start_copies(sources, targets, sems, first=0):
    copies = [
        pltpu.make_async_copy(source, target, sems.at[first + i])
        for i, (source, target) in enumerate(zip(sources, targets))
    ]
    for copy in copies:
        copy.start()
    return copies


def selections(place_ref, pick_ref, per_block, reals):
    block = lax.axis_index("blk")
    blocks, real_groups = lax.axis_size("blk"), lax.axis_size("real")
    modes, cycles, half = per_block * blocks, 2 * blocks, LANES // 2

    lane = lane_ids((1, LANES))
    row = row_ids((LANES, LANES))
    lane_order = (lane & (half - 1)) >> log2(cycles)
    lane_row = (lane & 1) * half + (lane >> log2(half)) * modes + block * per_block + lane_order
    pick_ref[0] = (row == lane_row).astype(jnp.float32).astype(jnp.bfloat16)
    lane_row = (lane >> log2(half)) * per_block + (lane & (per_block - 1))
    pick_ref[1] = ((row >> log2(cycles)) == lane_row).astype(jnp.float32).astype(jnp.bfloat16)

    spacing = reals + 2
    column = lane_ids((1, place_ref.shape[1]))
    source = (column * (2**16 // spacing + 1)) >> 16
    inside = column - source * spacing
    source_block = source >> log2(real_groups)
    target = ((source & (real_groups - 1)) * blocks + source_block) * reals + inside
    target = jnp.where(inside < reals, target, blocks * real_groups * reals + source_block)
    place = (row_ids(place_ref.shape) == target).astype(jnp.float32)
    place_ref[...] = place.astype(jnp.bfloat16)


def forward_kernel(
    cycle_len, half_len, syn_scale, reals,
    cycle_hbm, mode_hbm, noise_hbm, mask_hbm, spectrum_hbm, legendre_hbm, sky_hbm, prev_hbm,
    out_ref, inner_ref, outer_ref, place_ref, pick_ref, doubled_ref, factor_ref,
    cycle_ref, mode_ref, noise_ref, mask_ref, spectrum_ref, legendre_ref, sky_ref, prev_ref, gram_ref, sems,
):
    copies = start_copies(
        (cycle_hbm, mode_hbm, sky_hbm, prev_hbm, noise_hbm, mask_hbm, spectrum_hbm, legendre_hbm),
        (cycle_ref, mode_ref, sky_ref, prev_ref, noise_ref, mask_ref, spectrum_ref, legendre_ref),
        sems,
    )
    group = lax.axis_index("grp")
    per_block = legendre_ref.shape[0] // (2 * lax.axis_size("blk"))
    selections(place_ref, pick_ref, per_block, reals)
    copies[0].wait()
    copies[1].wait()
    inner, outer = phase_factors(cycle_ref[...], mode_ref[...], cycle_len, half_len, group)
    inner_ref[...] = inner
    outer_ref[...] = outer
    for copy in copies[2:]:
        copy.wait()
    weight = mask_ref[...].astype(jnp.float32) / (noise_ref[...] - 0.5)
    inverse = 1.0 / (weight + 2.0)
    sky_gain = weight * inverse
    prev_gain = 2.0 * inverse

    table = legendre_ref[...]
    spectrum = spectrum_ref[...]
    factor = spectrum / (spectrum + 0.5)
    doubled_ref[...] = jnp.concatenate([table, table], axis=0)
    factor_ref[...] = factor
    filtered = (table.astype(jnp.float32) * factor).astype(jnp.bfloat16)
    gram = lax.dot_general(table, filtered, NT, preferred_element_type=jnp.float32)
    table_rows = table.shape[0]
    pixel_rows = outer.shape[0]
    blocks, real_groups = lax.axis_size("blk"), lax.axis_size("real")
    cycles = 2 * blocks
    same = (row_ids(gram.shape) >> log2(cycles)) == (lane_ids((1, table_rows)) >> log2(cycles))
    gram = jnp.where(same, gram, 0.0).reshape(table_rows // cycles, cycles, table_rows).sum(axis=0)
    gram = gram * syn_scale
    gram_ref[...] = jnp.concatenate([gram, gram], axis=1)
    even, odd = gram_ref[pl.ds(0, blocks, stride=2), :], gram_ref[pl.ds(1, blocks, stride=2), :]
    gram = jnp.where(lane_ids(even.shape) < LANES // 2, even, odd)
    gram_high = gram.astype(jnp.bfloat16).astype(jnp.float32)
    gram_low = gram - gram_high

    shape = (reals, 2 * pixel_rows, LANES)
    messenger = sky_ref[...].reshape(shape) * sky_gain + prev_ref[...].reshape(shape) * prev_gain
    rows = jnp.concatenate([messenger[:, :pixel_rows], messenger[:, pixel_rows:]], axis=2)
    rows = rows.reshape(-1, 2 * LANES).astype(jnp.bfloat16)
    partial = jnp.dot(rows, inner, preferred_element_type=jnp.float32)
    partial = partial[:, :LANES] + partial[:, LANES:]
    turned = partial.reshape(reals, pixel_rows, LANES) * outer
    summed = turned.reshape(reals, pixel_rows // 8, 8, LANES).sum(axis=1)
    summed = summed.reshape(reals * 8, LANES)
    summed = summed + pltpu.roll(summed, LANES // 2, 1)
    own = (row_ids(summed.shape) & 1) == (lane_ids(summed.shape) >= LANES // 2)
    fourier = jnp.where(own, summed, 0.0).reshape(reals, 8, LANES).sum(axis=1) * cycle_len**-0.5
    rows = []
    for b in range(blocks):
        rows += [fourier, gram_high[b : b + 1], gram_low[b : b + 1]] * real_groups
    rows = jnp.concatenate(rows, axis=0).astype(jnp.bfloat16)
    for g in range(lax.axis_size("grp")):
        out_ref[pl.ds(g * rows.shape[0], rows.shape[0]), :] = rows


def backward_kernel(
    blocks, real_groups, reals, parts,
    gathered_ref, inner_ref, outer_ref, place_ref, pick_ref, table_ref, factor_ref,
    wiener_hbm, signal_hbm, wiener_ref, signal_ref, fourier_ref, out_sems,
):
    real_group = lax.axis_index("real")
    cycles = 2 * blocks
    per_block = table_ref.shape[0] // (2 * cycles)
    modes = per_block * blocks
    pixel_rows = outer_ref.shape[0]
    half = LANES // 2
    lane = lane_ids((1, LANES))
    holder = (lane & (modes - 1)) >> log2(per_block)
    lane_block = (lane & (cycles - 1)) >> 1
    total_reals = real_groups * reals
    fourier_rows = blocks * total_reals
    share = place_ref.shape[1]
    sides = jnp.concatenate([gathered_ref[:share, :], gathered_ref[share:, :]], axis=1)
    placed = jnp.dot(place_ref[...], sides, preferred_element_type=jnp.float32)
    placed = placed[:, :LANES] + placed[:, LANES:]
    fourier_ref[...] = placed[:fourier_rows]

    coeff_rows = jnp.dot(
        placed[:fourier_rows].astype(jnp.bfloat16), pick_ref[0], preferred_element_type=jnp.float32
    ).reshape(real_groups, blocks, reals, LANES)
    columns = jnp.zeros((total_reals, LANES), jnp.float32)
    for b in range(blocks):
        one = coeff_rows[:, b].reshape(total_reals, LANES)
        columns = columns + jnp.where(lane_block == b, one, 0.0)
    table = table_ref[...]
    factor = factor_ref[...]
    stores = []
    own = (lane >> log2(cycles)) == row_ids((2 * per_block, LANES))
    upper = row_ids((1, 2 * per_block, LANES)) < per_block
    pieces = jnp.where(own, columns[:, None, :], 0.0).reshape(-1, LANES).astype(jnp.bfloat16)
    filtered = factor * jnp.dot(pieces, table, preferred_element_type=jnp.float32)
    filtered = filtered.reshape(total_reals, 2 * per_block, -1)
    for y in range(real_groups):
        span = slice(y * reals, (y + 1) * reals)
        for pair in range(wiener_ref.shape[2]):
            one, two = (
                filtered[span, :, tile * LANES : (tile + 1) * LANES] for tile in (2 * pair, 2 * pair + 1)
            )
            wiener_ref[span, 0, pair] = jnp.where(upper, one, pltpu.roll(two, per_block, 1))
            wiener_ref[span, 1, pair] = jnp.where(upper, pltpu.roll(one, per_block, 1), two)
        span = pl.ds(y * reals, reals)
        stores += start_copies([wiener_ref.at[span]], [wiener_hbm.at[span]], out_sems, len(stores))

    gram_all = jnp.where(
        (lane & (cycles - 1)) == row_ids((cycles, LANES)), placed[fourier_rows:, None, :], 0.0
    ).reshape(blocks * cycles, LANES)
    gram_high = gram_all.astype(jnp.bfloat16)
    gram_low = (gram_all - gram_high.astype(jnp.float32)).astype(jnp.bfloat16)
    gram_rows = jnp.dot(
        jnp.concatenate([gram_high, gram_low], axis=1),
        jnp.concatenate([pick_ref[1], pick_ref[1]], axis=0),
        preferred_element_type=jnp.float32,
    ).reshape(blocks, cycles, LANES)
    gram = jnp.zeros((cycles, LANES), jnp.float32)
    for b in range(blocks):
        gram = gram + jnp.where(holder == b, gram_rows[b], 0.0)

    first = lane < half
    cycle_modes = jnp.zeros((reals, LANES), jnp.float32)
    for b in range(blocks):
        first_row = pl.multiple_of((real_group * blocks + b) * reals, reals)
        pair = fourier_ref[pl.ds(first_row, reals), :]
        turned = pltpu.roll(pair, half, 1)
        cycle_modes = cycle_modes + jnp.where(first, pair, turned) * gram[2 * b : 2 * b + 1]
        cycle_modes = cycle_modes + jnp.where(first, turned, pair) * gram[2 * b + 1 : 2 * b + 2]
    cycle_modes = cycle_modes * modes**-0.5
    turned = pltpu.roll(cycle_modes, half, 1)
    even = jnp.where(first, cycle_modes, turned)
    odd = jnp.where(first, turned, cycle_modes)
    parity = (row_ids((1, 8, LANES)) & 1) == 0
    spread = jnp.where(parity, even[:, None, :], odd[:, None, :])
    inner = inner_ref[...]
    outer = outer_ref[...].reshape(1, pixel_rows // 8, 8, LANES)
    rotated = (spread[:, None] * outer).reshape(-1, LANES).astype(jnp.bfloat16)
    signal = lax.dot_general(
        jnp.concatenate([rotated, rotated], axis=1), inner, NT, preferred_element_type=jnp.float32
    ).reshape(reals, pixel_rows, 2 * LANES)
    part_reals = reals // parts
    for i in range(parts):
        span = slice(i * part_reals, (i + 1) * part_reals)
        signal_ref[span, 0] = signal[span, :, :LANES]
        signal_ref[span, 1] = signal[span, :, LANES:]
        span = pl.ds(i * part_reals, part_reals)
        stores += start_copies([signal_ref.at[span]], [signal_hbm.at[span]], out_sems, len(stores))
    for store in stores:
        store.wait()


def split_tiles(array):
    lead, rows, columns = array.shape[:-2], array.shape[-2], array.shape[-1]
    split = array.reshape(*lead, rows, columns // LANES, LANES)
    return jnp.swapaxes(split, -2, -3).reshape(-1, LANES)


def gram_program(
    sky_data, signal_prev, noise_var, mask_flags, cycle_table, m_table, spectrum, legendre
):
    reals, cycle_dev, half_len = sky_data.shape
    groups, blocks, real_groups = (lax.axis_size(name) for name in AXES)
    cycle_len = half_len * groups
    per_block, multipoles, cycles = legendre.shape
    total_l = multipoles * groups * real_groups
    tiles = multipoles // LANES
    hbm = pl.BlockSpec(memory_space=pltpu.HBM)
    vmem = pl.BlockSpec(memory_space=pltpu.VMEM)
    orders = m_table[None, :]
    cycles_row = cycle_table[None, :]
    spectrum_row = spectrum[None, :]
    table = legendre.transpose(0, 2, 1).reshape(per_block * cycles, multipoles)
    inputs = (
        cycles_row, orders, split_tiles(noise_var), split_tiles(mask_flags), spectrum_row, table,
        split_tiles(sky_data), split_tiles(signal_prev),
    )
    sources = groups * blocks * real_groups
    total_reals = reals * real_groups
    local, *prepared = pl.pallas_call(
        functools.partial(forward_kernel, cycle_len, half_len, (cycles / total_l) ** 0.5, reals),
        out_shape=(
            jax.ShapeDtypeStruct((sources * (reals + 2), LANES), jnp.bfloat16),
            jax.ShapeDtypeStruct((2 * LANES, 2 * LANES), jnp.bfloat16),
            jax.ShapeDtypeStruct((half_len // LANES, LANES), jnp.float32),
            jax.ShapeDtypeStruct(
                (blocks * (total_reals + 1), blocks * real_groups * (reals + 2)), jnp.bfloat16
            ),
            jax.ShapeDtypeStruct((2, LANES, LANES), jnp.bfloat16),
            jax.ShapeDtypeStruct((2 * table.shape[0], multipoles), jnp.bfloat16),
            jax.ShapeDtypeStruct((1, multipoles), jnp.float32),
        ),
        in_specs=[hbm] * 8,
        out_specs=(vmem,) * 7,
        scratch_shapes=[pltpu.VMEM(x.shape, x.dtype) for x in inputs]
        + [pltpu.VMEM((cycles, LANES), jnp.float32), pltpu.SemaphoreType.DMA((8,))],
        compiler_params=pltpu.CompilerParams(vmem_limit_bytes=FORWARD_VMEM),
    )(*(pltpu.with_memory_space_constraint(x, pltpu.HBM) for x in inputs))
    pairs = local.reshape(sources, reals // 2 + 1, 2, LANES)
    gathered = lax.all_to_all(pairs, AXES, 0, 0, tiled=True).reshape(local.shape)
    outputs = (
        jax.ShapeDtypeStruct((total_reals, 2, tiles // 2, 2 * per_block, LANES), jnp.float32),
        jax.ShapeDtypeStruct((reals, 2, half_len // LANES, LANES), jnp.float32),
    )
    wiener, signal = pl.pallas_call(
        functools.partial(backward_kernel, blocks, real_groups, reals, PARTS),
        out_shape=outputs,
        in_specs=[vmem] * 7,
        out_specs=(hbm, hbm),
        scratch_shapes=[pltpu.VMEM(x.shape, x.dtype) for x in outputs]
        + [pltpu.VMEM((blocks * total_reals, LANES), jnp.float32)]
        + [pltpu.SemaphoreType.DMA((real_groups + PARTS,))],
        compiler_params=pltpu.CompilerParams(vmem_limit_bytes=BACKWARD_VMEM),
    )(gathered, *prepared)
    wiener = wiener.reshape(total_reals, 2, tiles, per_block, LANES).transpose(0, 1, 3, 2, 4)
    signal = signal.reshape(reals, half_len // LANES, cycle_dev, LANES).transpose(0, 2, 1, 3)
    return (
        wiener.reshape(total_reals, 2, per_block, multipoles),
        signal.reshape(sky_data.shape),
    )


def gram_form_fits(mesh, sky_data, m_table, legendre):
    groups, blocks, real_groups = (mesh.shape[name] for name in AXES)
    reals, cycles, cycle_len = sky_data.shape
    modes = m_table.shape[0]
    per_block = modes // blocks
    multipoles = legendre.shape[1] // (groups * real_groups)
    half_len = cycle_len // groups
    reals_dev = reals // real_groups
    return (
        cycles < 2 * reals
        and 4 * modes == LANES
        and cycles == 2 * blocks
        and all(size & (size - 1) == 0 for size in (blocks, modes, cycles, real_groups))
        and 2 * reals * cycles < 2**12
        and 2 * per_block * cycles == LANES
        and cycle_len & (cycle_len - 1) == 0
        and half_len % (8 * LANES) == 0
        and multipoles % (2 * LANES) == 0
        and per_block == 4
        and reals_dev % 16 == 0
        and reals_dev % PARTS == 0
        and cycles % 16 == 0
    )


def phase_tables(col_ids, mode_ids, cycle_len):
    product_ids = col_ids[:, None] * mode_ids[None, :] % cycle_len
    angles = product_ids.astype(jnp.float32) * (2.0 * math.pi / cycle_len)
    return (jnp.cos(angles).astype(jnp.bfloat16), jnp.sin(angles).astype(jnp.bfloat16))


def cycle_offsets(cycle_ids, mode_ids, cycle_len):
    parity = (cycle_ids % 2).astype(jnp.float32)
    shifts = math.pi / cycle_len * parity[:, None] * mode_ids[None, :].astype(jnp.float32)
    return (jnp.cos(shifts), jnp.sin(shifts))


def forward_modes(re_part, im_part):
    summed = lax.psum((re_part, im_part), "grp")
    fourier_pair = (summed[0].astype(jnp.bfloat16), summed[1].astype(jnp.bfloat16))
    fourier_pair = (
        lax.all_gather(fourier_pair[0], "real", axis=0, tiled=True),
        lax.all_gather(fourier_pair[1], "real", axis=0, tiled=True),
    )
    fourier_pair = (
        lax.all_to_all(fourier_pair[0], "blk", split_axis=2, concat_axis=1, tiled=True),
        lax.all_to_all(fourier_pair[1], "blk", split_axis=2, concat_axis=1, tiled=True),
    )
    return fourier_pair


def backward_cycles(partial_value):
    summed = lax.psum_scatter(partial_value, "real", scatter_dimension=0, tiled=True)
    reduced = lax.psum(summed, "grp")
    cycle_pair = lax.all_to_all(
        reduced.astype(jnp.bfloat16), "blk", split_axis=2, concat_axis=3, tiled=True
    )
    return cycle_pair


def per_device(
    sky_data, signal_prev, noise_var, mask_flags, cycle_table, m_table, spectrum, legendre
):
    real_dev, cycle_dev, half_len = sky_data.shape
    cycle_len = half_len * lax.axis_size("grp")
    mode_count = m_table.shape[0]
    col_ids = lax.axis_index("grp") * half_len + jnp.arange(half_len, dtype=jnp.int32)
    cos_tab, sin_tab = phase_tables(col_ids, m_table, cycle_len)
    cos_shift, sin_shift = cycle_offsets(cycle_table, m_table, cycle_len)
    weight = mask_flags.astype(jnp.float32) / (noise_var - 0.5)
    messenger = (weight * sky_data + 2.0 * signal_prev) / (weight + 2.0)
    flat_rows = messenger.astype(jnp.bfloat16).reshape(real_dev * cycle_dev, half_len)
    base_cos = jnp.dot(flat_rows, cos_tab, preferred_element_type=jnp.float32).reshape(
        real_dev, cycle_dev, mode_count
    )
    base_sin = -jnp.dot(flat_rows, sin_tab, preferred_element_type=jnp.float32).reshape(
        real_dev, cycle_dev, mode_count
    )
    norm_scale = cycle_len ** (-0.5)
    re_part = (base_cos * cos_shift + base_sin * sin_shift) * norm_scale
    im_part = (base_sin * cos_shift - base_cos * sin_shift) * norm_scale
    fourier_re, fourier_im = forward_modes(re_part, im_part)
    fourier = jnp.stack([fourier_re, fourier_im], 1)
    coefficients = jnp.einsum(
        "mlr,kcrm->kcml", legendre, fourier, preferred_element_type=jnp.float32
    )
    factor = spectrum / (spectrum + 0.5)
    wiener_alm = coefficients * factor
    total_l = legendre.shape[1] * lax.axis_size("grp") * lax.axis_size("real")
    syn_scale = (legendre.shape[2] / total_l) ** 0.5
    partial_value = (
        jnp.einsum(
            "mlr,kcml->kcrm",
            legendre,
            wiener_alm.astype(jnp.bfloat16),
            preferred_element_type=jnp.float32,
        )
        * syn_scale
    )
    cycle_pair = backward_cycles(partial_value)
    cycle_modes = cycle_pair.astype(jnp.float32)
    modes_re = cycle_modes[:, 0]
    modes_im = cycle_modes[:, 1]
    rotated_re = (modes_re * cos_shift - modes_im * sin_shift).astype(jnp.bfloat16)
    rotated_im = (modes_im * cos_shift + modes_re * sin_shift).astype(jnp.bfloat16)
    contract = (((1,), (1,)), ((), ()))
    pixel_sum = lax.dot_general(
        rotated_re.reshape(-1, mode_count), cos_tab, contract, preferred_element_type=jnp.float32
    )
    pixel_sum = pixel_sum - lax.dot_general(
        rotated_im.reshape(-1, mode_count), sin_tab, contract, preferred_element_type=jnp.float32
    )
    signal_next = (pixel_sum * mode_count ** (-0.5)).reshape(real_dev, cycle_dev, half_len)
    return (wiener_alm, signal_next)


def solution(mesh):
    in_specs = (
        P("real", "blk", "grp"),
        P("real", "blk", "grp"),
        P("blk", "grp"),
        P("blk", "grp"),
        P("blk"),
        P(),
        P(("grp", "real")),
        P("blk", ("grp", "real"), None),
    )
    out_specs = (P(None, None, "blk", ("grp", "real")), P("real", "blk", "grp"))

    def step(sky_data, signal_prev, noise_var, mask_flags, cycle_table, m_table, spectrum, legendre):
        fits = gram_form_fits(mesh, sky_data, m_table, legendre)
        return jax.shard_map(
            gram_program if fits else per_device,
            mesh=mesh,
            in_specs=in_specs,
            out_specs=out_specs,
            check_vma=False,
        )(sky_data, signal_prev, noise_var, mask_flags, cycle_table, m_table, spectrum, legendre)

    return step
```

profile of v0, /device:TPU:0, one launch (start us, length us, event | category | flops | bytes accessed | tf_op | source)
XLA Modules:
  0.0 19.5 jit_solution(4958250106690822516)
XLA Ops:
  0.6 1.8 %shard_map.95 = (bf16[576,128]{1,0:T(8,128)(2,1)S(1)}, bf16[256,256]{1,0:T(8,128)(2,1)S(1)}, f32[32,128]{1,0:T(8,128)S(1)}, bf16[264,288]{1,0:T(8,128)(2,1)S(1)}...) custom-call(s32[1,2]{1,0:T(1,128)} %bitcast.46, s32[1,32]{1,0:T(1,128)} %bitcast.47, ...), custom_call_target="tpu_custom_call" | custom-call | tf_op jit(solution)/shard_map/pallas_call | solution.py:282
  2.4 15.3 %all_to_all.5 = bf16[32,9,2,128]{3,2,1,0:T(2,128)(2,1)S(1)} all-to-all(bf16[32,9,2,128]{3,2,1,0:T(2,128)(2,1)S(1)} %bitcast.39), channel_id=1, replica_groups=mesh['grp'=2,'blk'=8,'real'=2] {'grp','blk','real'}, dimensions={0} | all-to-all | bytes 294912 | tf_op jit(solution)/shard_map/all_to_all | solution.py:302
  17.7 1.8 %shard_map.96 = (f32[32,2,4,8,128]{4,3,2,1,0:T(8,128)}, f32[16,2,32,128]{3,2,1,0:T(8,128)}) custom-call(bf16[576,128]{1,0:T(8,128)(2,1)S(1)} %bitcast.38, bf16[256,256]{1,0:T(8,128)(2,1)S(1)} %get-tuple-element.12.inner_ref, f32[32,128]{1,0:T(8,128)S(1)} %get-tuple-element.13.outer_ref, bf16[264,288]{1,0:T(8,128)(2,1)S(1)} %get-tuple-element.14.place_ref, ...), custom_call_target="tpu_custom_call" | custom-call | tf_op jit(solution)/shard_map/pallas_call | solution.py:307
where the time goes:
time: 19.7 us; the launch traced here: 19.5 us
  blocking collectives  15.3 us (78%)
  Pallas kernels  3.59 us (18%)
  between operations  0.64 us (3%)
    all_to_all x1, blocking collectives, gram_program(): lax.all_to_all(pairs, AXES, 0, 0, tiled=True).reshape(local.shape)  15.3 us
    pallas_call x1, Pallas kernels, gram_program(): pl.pallas_call(functools.partial(backward_kernel, blocks, real_groups, re...  1.82 us
    pallas_call x1, Pallas kernels, gram_program(): pl.pallas_call(functools.partial(forward_kernel, cycle_len, half_len, (cy...  1.77 us

commit v1 on v0

--- a/solution.py
+++ b/solution.py
@@ -86,8 +86,8 @@
     column = lane_ids((1, place_ref.shape[1]))
     source = (column * (2**16 // spacing + 1)) >> 16
     inside = column - source * spacing
-    source_block = source >> log2(real_groups)
-    target = ((source & (real_groups - 1)) * blocks + source_block) * reals + inside
+    source_block = source & (blocks - 1)
+    target = source * reals + inside
     target = jnp.where(inside < reals, target, blocks * real_groups * reals + source_block)
     place = (row_ids(place_ref.shape) == target).astype(jnp.float32)
     place_ref[...] = place.astype(jnp.bfloat16)
@@ -153,8 +153,8 @@
     fourier = jnp.where(own, summed, 0.0).reshape(reals, 8, LANES).sum(axis=1) * cycle_len**-0.5
     rows = []
     for b in range(blocks):
-        rows += [fourier, gram_high[b : b + 1], gram_low[b : b + 1]] * real_groups
-    rows = jnp.concatenate(rows, axis=0).astype(jnp.bfloat16)
+        rows += [fourier, gram_high[b : b + 1], gram_low[b : b + 1]]
+    rows = jnp.concatenate(rows * real_groups, axis=0).astype(jnp.bfloat16)
     for g in range(lax.axis_size("grp")):
         out_ref[pl.ds(g * rows.shape[0], rows.shape[0]), :] = rows
 
@@ -299,7 +299,7 @@
         compiler_params=pltpu.CompilerParams(vmem_limit_bytes=FORWARD_VMEM),
     )(*(pltpu.with_memory_space_constraint(x, pltpu.HBM) for x in inputs))
     pairs = local.reshape(sources, reals // 2 + 1, 2, LANES)
-    gathered = lax.all_to_all(pairs, AXES, 0, 0, tiled=True).reshape(local.shape)
+    gathered = lax.all_to_all(pairs, ("grp", "real", "blk"), 0, 0, tiled=True).reshape(local.shape)
     outputs = (
         jax.ShapeDtypeStruct((total_reals, 2, tiles // 2, 2 * per_block, LANES), jnp.float32),
         jax.ShapeDtypeStruct((reals, 2, half_len // LANES, LANES), jnp.float32),

time: 19.7 us -> 19.6 us (level)
  no operation moved by 1% of the time
where the time goes in v1:
time: 19.6 us; the launch traced here: 19.5 us
  blocking collectives  15.2 us (78%)
  Pallas kernels  3.59 us (18%)
  between operations  0.64 us (3%)
    all_to_all x1, blocking collectives, gram_program(): lax.all_to_all(pairs, ('grp', 'real', 'blk'), 0, 0, tiled=True)  15.2 us
    pallas_call x1, Pallas kernels, gram_program(): pl.pallas_call(functools.partial(backward_kernel, blocks, real_groups, re...  1.82 us
    pallas_call x1, Pallas kernels, gram_program(): pl.pallas_call(functools.partial(forward_kernel, cycle_len, half_len, (cy...  1.76 us

profile of v1, /device:TPU:0, one launch (start us, length us, event | category | flops | bytes accessed | tf_op | source)
XLA Modules:
  0.0 19.5 jit_solution(11060995997921195462)
XLA Ops:
  0.6 1.8 %shard_map.95 = (bf16[576,128]{1,0:T(8,128)(2,1)S(1)}, bf16[256,256]{1,0:T(8,128)(2,1)S(1)}, f32[32,128]{1,0:T(8,128)S(1)}, bf16[264,288]{1,0:T(8,128)(2,1)S(1)}...) custom-call(s32[1,2]{1,0:T(1,128)} %bitcast.46, s32[1,32]{1,0:T(1,128)} %bitcast.47, ...), custom_call_target="tpu_custom_call" | custom-call | tf_op jit(solution)/shard_map/pallas_call | solution.py:282
  2.4 15.2 %all_to_all.5 = bf16[32,9,2,128]{3,2,1,0:T(2,128)(2,1)S(1)} all-to-all(bf16[32,9,2,128]{3,2,1,0:T(2,128)(2,1)S(1)} %bitcast.39), channel_id=1, replica_groups=mesh['grp'=2,'blk'=8,'real'=2] {'grp','real','blk'}, dimensions={0} | all-to-all | bytes 294912 | tf_op jit(solution)/shard_map/all_to_all | solution.py:302
  17.6 1.8 %shard_map.96 = (f32[32,2,4,8,128]{4,3,2,1,0:T(8,128)}, f32[16,2,32,128]{3,2,1,0:T(8,128)}) custom-call(bf16[576,128]{1,0:T(8,128)(2,1)S(1)} %bitcast.38, bf16[256,256]{1,0:T(8,128)(2,1)S(1)} %get-tuple-element.12.inner_ref, f32[32,128]{1,0:T(8,128)S(1)} %get-tuple-element.13.outer_ref, bf16[264,288]{1,0:T(8,128)(2,1)S(1)} %get-tuple-element.14.place_ref, ...), custom_call_target="tpu_custom_call" | custom-call | tf_op jit(solution)/shard_map/pallas_call | solution.py:307
